TPU v7x, 32 devices: a whole 2x2x4 slice. The times are simulated.
32 devices in a mesh: section: 2 (over x), dp: 16 (over z, y, core).
Axes of the slice: x: 2, y: 2, z: 4, core: 2. Of those that a mesh axis runs over, the one named last changes fastest.
Arguments:
- content_in: bfloat16 [2, 4096, 768], P(None, 'dp'), may hold values from -6 to 6
- query_in: bfloat16 [2, 4096, 768], P(None, 'dp'), may hold values from -6 to 6
- content_cot: bfloat16 [2, 4096, 768], P(None, 'dp'), may hold values from -6 to 6
- query_cot: bfloat16 [2, 4096, 768], P(None, 'dp'), may hold values from -6 to 6
- lengths: int32 [2, 16, 16], P(None, 'dp'), may hold values from 0 to 256, as said below
- order: int32 [2, 4096], P(None, 'dp'), may hold values from 0 to 4095, each once within a row
- predicted: int32 [2, 4096], P(None, 'dp'), may hold values 0 or 1
- proj_weight: bfloat16 [2, 3, 768, 768], P('section'), may hold values from -0.21875 to 0.21875
- out_weight: bfloat16 [2, 768, 768], P('section'), may hold values from -0.875 to 0.875
- up_weight: bfloat16 [2, 768, 3072], P('section'), may hold values from -0.21875 to 0.21875
- down_weight: bfloat16 [2, 3072, 768], P('section'), may hold values from -0.109375 to 0.109375
- up_bias: float32 [2, 3072], P('section'), may hold values from -3 to 3
- biases: float32 [2, 6, 768], P('section'), may hold values from -3 to 3
- gains: float32 [2, 2, 768], P('section'), may hold values from 0.5 to 1.5
- rel_table: float32 [2, 384], P('section'), may hold values from -5 to 5
Outputs:
- content_out: bfloat16 [2, 2, 4096, 768], P('section', None, 'dp')
- query_out: bfloat16 [2, 2, 4096, 768], P('section', None, 'dp')
- content_grad: bfloat16 [2, 2, 4096, 768], P('section', None, 'dp')
- query_grad: bfloat16 [2, 2, 4096, 768], P('section', None, 'dp')
- proj_grad: float32 [2, 3, 768, 768], P('section', None, 'dp')
- out_grad: float32 [2, 768, 768], P('section', 'dp')
- up_grad: float32 [2, 768, 3072], P('section', 'dp')
- down_grad: float32 [2, 3072, 768], P('section', 'dp')
- up_bias_grad: float32 [2, 3072], P('section', 'dp')
- biases_grad: float32 [2, 6, 768], P('section', None, 'dp')
- gains_grad: float32 [2, 2, 768], P('section', None, 'dp')
- table_grad: float32 [2, 384], P('section', 'dp')
Inputs may be any that keep to these rules, and one draw needn't show every extreme that they name: Each row of 16 lengths (one micro-batch, one index of dp) lists sequences of one token or more first and zeros after them; a row sums to 224 or more and to 256 at most; in every draw some row is one sequence of 256 tokens. `order`: within a micro-batch every token has a rank of its own.
All inputs are finite; a program needn't handle non-finite values. No bound on the sum of `predicted` on one device may be relied on, other than what follows from the above.
Results may differ from a plain program's by a relative error of at most 0.03.
Values may be sent and summed in bfloat16 or wider, within the bound.
No kernel may reach another device: no remote copies, remote signals or barrier semaphores. Data moves between devices by JAX's collectives and lax.ppermute only.
A program may use at most 320 MiB of HBM per device.

v0:
```python
from functools import partial

import jax
import jax.numpy as jnp
from jax import lax
from jax.sharding import PartitionSpec as P

NEG_FILL = -1e30
LN_EPS = 1e-05
BUCKET_EDGES = (12, 16, 23, 32, 46, 64, 91)


def for_sending(shard):

    def short(part):
        return part.astype(jnp.bfloat16) if part.dtype == jnp.float32 else part

    return jax.tree.map(short, shard)


def from_behind(block, axis, distance):
    devices = range(lax.axis_size(axis))
    route = [(i - distance, i) for i in devices if i - distance in devices]
    return lax.ppermute(block, axis, route)


def layer_norm(values, gain_vec, shift_vec):
    center = values - jnp.mean(values, axis=-1, keepdims=True)
    spread = jnp.mean(center * center, axis=-1, keepdims=True)
    return center * lax.rsqrt(spread + LN_EPS) * gain_vec + shift_vec


def bucket_index(relative):
    magnitude = jnp.abs(relative)
    far_part = jnp.full_like(magnitude, 8)
    for edge_at in BUCKET_EDGES:
        far_part = far_part + (magnitude >= edge_at).astype(jnp.int32)
    near_far = jnp.where(magnitude < 8, magnitude, far_part)
    return near_far + 16 * (relative > 0).astype(jnp.int32)


def layout(length_row, order_row, predicted_row):
    row_count = order_row.shape[0]
    tokens_idx = jnp.arange(row_count, dtype=jnp.int32)
    seq_ends = jnp.cumsum(length_row)
    passed = tokens_idx[:, None] >= seq_ends[None, :]
    segment = jnp.sum(passed.astype(jnp.int32), axis=1)
    starts = jnp.sum(jnp.where(passed, length_row[None, :], 0), axis=1)
    inside = tokens_idx < seq_ends[-1]
    position = jnp.where(inside, tokens_idx - starts, 0)
    segment = jnp.where(inside, segment, -1 - tokens_idx)
    masked_tok = (predicted_row > 0) & inside & (position > 0)
    same_seq = segment[:, None] == segment[None, :]
    shown_key = jnp.logical_not(masked_tok)[None, :]
    earlier_eq = order_row[None, :] <= order_row[:, None]
    earlier = order_row[None, :] < order_row[:, None]
    see_content = same_seq & (shown_key | earlier_eq)
    see_query = same_seq & (shown_key | earlier)
    buckets = bucket_index(position[None, :] - position[:, None])
    return (see_content, see_query, buckets)


def matmul(left, right):
    return jnp.dot(left, right, preferred_element_type=jnp.float32)


def contract_rows(left, right):
    return jnp.einsum("ra,rb->ab", left, right, preferred_element_type=jnp.float32)


def times_transpose(left, right):
    return jnp.einsum("ra,ba->rb", left, right, preferred_element_type=jnp.float32)


def attend(queries, key_heads, value_heads, rel_bias, visible):
    row_count = queries.shape[0]
    head_count = rel_bias.shape[0]
    query_split = queries.reshape(row_count, head_count, -1)
    key_split = key_heads.reshape(row_count, head_count, -1)
    value_split = value_heads.reshape(row_count, head_count, -1)
    raw_scores = (
        jnp.einsum("qhe,khe->hqk", query_split, key_split, preferred_element_type=jnp.float32)
        * 0.125
        + rel_bias
    )
    logits = jnp.where(visible[None], raw_scores, NEG_FILL)
    row_max = jnp.max(logits, axis=-1, keepdims=True)
    exp_scores = jnp.exp(logits - row_max)
    softmaxed = exp_scores / jnp.sum(exp_scores, axis=-1, keepdims=True)
    soft_low = softmaxed.astype(jnp.bfloat16)
    mixed_out = jnp.einsum(
        "hqk,khe->qhe", soft_low, value_split, preferred_element_type=jnp.float32
    )
    return (softmaxed, soft_low, mixed_out.reshape(row_count, -1).astype(jnp.bfloat16))


def layer_forward(content, query, weights, visibility):
    projections, out_proj, up_proj, down_proj, up_shift, bias_rows, gain_rows, table_flat = weights
    see_content, see_query, buckets = visibility
    row_count = content.shape[0]
    head_count = table_flat.shape[0] // 32
    onehot = (buckets.reshape(-1)[:, None] == jnp.arange(32, dtype=jnp.int32)[None, :]).astype(
        jnp.float32
    )
    rel_bias = jnp.dot(
        onehot, table_flat.reshape(32, head_count), precision=lax.Precision.HIGHEST
    ).T.reshape(head_count, row_count, row_count)
    key_heads = matmul(content, projections[1]).astype(jnp.bfloat16)
    value_heads = (matmul(content, projections[2]) + bias_rows[1]).astype(jnp.bfloat16)
    streams = []
    for inputs, visible in ((content, see_content), (query, see_query)):
        queries = (matmul(inputs, projections[0]) + bias_rows[0]).astype(jnp.bfloat16)
        softmaxed, soft_low, mixed_out = attend(queries, key_heads, value_heads, rel_bias, visible)
        summed = inputs.astype(jnp.float32) + (matmul(mixed_out, out_proj) + bias_rows[2])
        normed = layer_norm(summed, gain_rows[0], bias_rows[4])
        normed_low = normed.astype(jnp.bfloat16)
        inner_pre = matmul(normed_low, up_proj) + up_shift
        act_low = jax.nn.gelu(inner_pre, approximate=False).astype(jnp.bfloat16)
        total_sum = normed + (matmul(act_low, down_proj) + bias_rows[3])
        result = layer_norm(total_sum, gain_rows[1], bias_rows[5]).astype(jnp.bfloat16)
        streams.append(
            (
                result,
                inputs,
                queries,
                softmaxed,
                soft_low,
                mixed_out,
                summed,
                normed_low,
                inner_pre,
                act_low,
                total_sum,
            )
        )
    return (streams, key_heads, value_heads, onehot)


def forward_only(content, query, weights, visibility):
    streams = layer_forward(content, query, weights, visibility)[0]
    return (streams[0][0], streams[1][0])


def forward_backward(content, query, content_up, query_up, weights, visibility, ffn_hook=None):
    streams, key_heads, value_heads, onehot = layer_forward(content, query, weights, visibility)
    projections, out_proj, up_proj, down_proj, up_shift, bias_rows, gain_rows, table_flat = weights
    row_count = content.shape[0]
    head_count = table_flat.shape[0] // 32
    key_split = key_heads.reshape(row_count, head_count, -1)
    value_split = value_heads.reshape(row_count, head_count, -1)
    grad_key = jnp.zeros(key_split.shape, jnp.float32)
    grad_value = jnp.zeros(value_split.shape, jnp.float32)
    score_total = jnp.zeros((head_count, row_count, row_count), jnp.float32)
    grad_query_proj = 0.0
    grad_out = 0.0
    grad_up = 0.0
    grad_down = 0.0
    grad_up_shift = 0.0
    grad_query_shift = 0.0
    grad_out_shift = 0.0
    grad_ffn_shift = 0.0
    grad_shift_one = 0.0
    grad_shift_two = 0.0
    grad_gain_one = 0.0
    grad_gain_two = 0.0
    input_grads = []
    hooked = None
    for stream_idx, (stream_data, upstream) in enumerate(zip(streams, (content_up, query_up))):
        (
            result,
            inputs,
            queries,
            softmaxed,
            soft_low,
            mixed_out,
            summed,
            normed_low,
            inner_pre,
            act_low,
            total_sum,
        ) = stream_data
        ln_value, ln_pull = jax.vjp(layer_norm, total_sum, gain_rows[1], bias_rows[5])
        d_total, d_gain_two, d_shift_two = ln_pull(upstream.astype(jnp.float32))
        grad_gain_two = grad_gain_two + d_gain_two
        grad_shift_two = grad_shift_two + d_shift_two
        d_ffn = d_total.astype(jnp.bfloat16)
        grad_down = grad_down + contract_rows(act_low, d_ffn)
        grad_ffn_shift = grad_ffn_shift + jnp.sum(d_ffn.astype(jnp.float32), axis=0)
        d_act = times_transpose(d_ffn, down_proj)
        gelu_value, gelu_pull = jax.vjp(partial(jax.nn.gelu, approximate=False), inner_pre)
        d_inner = gelu_pull(d_act)[0].astype(jnp.bfloat16)
        grad_up = grad_up + contract_rows(normed_low, d_inner)
        grad_up_shift = grad_up_shift + jnp.sum(d_inner.astype(jnp.float32), axis=0)
        d_normed = d_total + times_transpose(d_inner, up_proj)
        norm_value, norm_pull = jax.vjp(layer_norm, summed, gain_rows[0], bias_rows[4])
        d_summed, d_gain_one, d_shift_one = norm_pull(d_normed)
        grad_gain_one = grad_gain_one + d_gain_one
        grad_shift_one = grad_shift_one + d_shift_one
        d_branch = d_summed.astype(jnp.bfloat16)
        grad_out = grad_out + contract_rows(mixed_out, d_branch)
        grad_out_shift = grad_out_shift + jnp.sum(d_branch.astype(jnp.float32), axis=0)
        d_mixed = (
            times_transpose(d_branch, out_proj)
            .astype(jnp.bfloat16)
            .reshape(row_count, head_count, -1)
        )
        d_soft = jnp.einsum(
            "qhe,khe->hqk", d_mixed, value_split, preferred_element_type=jnp.float32
        )
        grad_value = grad_value + jnp.einsum(
            "hqk,qhe->khe", soft_low, d_mixed, preferred_element_type=jnp.float32
        )
        row_dot = jnp.sum(softmaxed * d_soft, axis=-1, keepdims=True)
        d_scores = (softmaxed * (d_soft - row_dot)).astype(jnp.bfloat16)
        score_total = score_total + d_scores.astype(jnp.float32)
        query_split = queries.reshape(row_count, head_count, -1)
        d_queries = (
            (
                jnp.einsum("hqk,khe->qhe", d_scores, key_split, preferred_element_type=jnp.float32)
                * 0.125
            )
            .reshape(row_count, -1)
            .astype(jnp.bfloat16)
        )
        grad_key = (
            grad_key
            + jnp.einsum("hqk,qhe->khe", d_scores, query_split, preferred_element_type=jnp.float32)
            * 0.125
        )
        grad_query_proj = grad_query_proj + contract_rows(inputs, d_queries)
        grad_query_shift = grad_query_shift + jnp.sum(d_queries.astype(jnp.float32), axis=0)
        input_grads.append(d_summed + times_transpose(d_queries, projections[0]))
    d_keys = grad_key.reshape(row_count, -1).astype(jnp.bfloat16)
    d_values = grad_value.reshape(row_count, -1).astype(jnp.bfloat16)
    grad_key_proj = contract_rows(content, d_keys)
    grad_value_proj = contract_rows(content, d_values)
    grad_value_shift = jnp.sum(d_values.astype(jnp.float32), axis=0)
    content_back = (
        input_grads[0]
        + times_transpose(d_keys, projections[1])
        + times_transpose(d_values, projections[2])
    )
    grad_table = jnp.dot(
        onehot.T, score_total.reshape(head_count, -1).T, precision=lax.Precision.HIGHEST
    ).reshape(-1)
    grad_parts = (
        jnp.stack([grad_query_proj, grad_key_proj, grad_value_proj]),
        grad_out,
        grad_up,
        grad_down,
        grad_up_shift,
        jnp.stack(
            [
                grad_query_shift,
                grad_value_shift,
                grad_out_shift,
                grad_ffn_shift,
                grad_shift_one,
                grad_shift_two,
            ]
        ),
        jnp.stack([grad_gain_one, grad_gain_two]),
        grad_table,
    )
    outcome = (
        streams[0][0],
        streams[1][0],
        content_back.astype(jnp.bfloat16),
        input_grads[1].astype(jnp.bfloat16),
        grad_parts,
    )
    return outcome


def body(
    content_in,
    query_in,
    content_cot,
    query_cot,
    lengths,
    order,
    predicted,
    proj_weight,
    out_weight,
    up_weight,
    down_weight,
    up_bias,
    biases,
    gains,
    rel_table,
):
    micro_count = content_in.shape[0]
    first_section = lax.axis_index("section") == 0
    select_section = partial(jnp.where, first_section)
    weights = (
        proj_weight[0],
        out_weight[0],
        up_weight[0],
        down_weight[0],
        up_bias[0],
        biases[0],
        gains[0],
        rel_table[0],
    )
    layouts = [
        layout(lengths[micro_idx, 0], order[micro_idx], predicted[micro_idx])
        for micro_idx in range(micro_count)
    ]
    blank_rows = jnp.zeros(content_in.shape[1:], jnp.bfloat16)
    blank_grads = tuple((jnp.zeros(member.shape, jnp.float32) for member in weights))
    section_outputs = []
    section_inputs = []
    for micro_idx in range(micro_count):
        made_pair = lax.cond(
            first_section,
            partial(
                forward_only,
                content_in[micro_idx],
                query_in[micro_idx],
                weights,
                layouts[micro_idx],
            ),
            lambda: (blank_rows, blank_rows),
        )
        section_outputs.append(made_pair)
        section_inputs.append(
            from_behind((for_sending(made_pair[0]), for_sending(made_pair[1])), "section", 1)
        )
    returned_grads = (blank_rows, blank_rows)
    tick_results = []
    grad_totals = blank_grads
    for tick_idx in range(micro_count + 1):
        late_idx = min(tick_idx, micro_count - 1)
        early_idx = max(tick_idx - 1, 0)
        active = jnp.where(first_section, tick_idx >= 1, tick_idx < micro_count)
        content_now = select_section(content_in[early_idx], section_inputs[late_idx][0])
        query_now = select_section(query_in[early_idx], section_inputs[late_idx][1])
        content_up = select_section(returned_grads[0], content_cot[late_idx])
        query_up = select_section(returned_grads[1], query_cot[late_idx])
        visibility = tuple(
            (
                select_section(early_part, late_part)
                for early_part, late_part in zip(layouts[early_idx], layouts[late_idx])
            )
        )
        tick_out = lax.cond(
            active,
            partial(
                forward_backward, content_now, query_now, content_up, query_up, weights, visibility
            ),
            lambda: (blank_rows, blank_rows, blank_rows, blank_rows, blank_grads),
        )
        tick_results.append(tick_out)
        if tick_idx < micro_count:
            returned_grads = from_behind(
                (for_sending(tick_out[2]), for_sending(tick_out[3])), "section", -1
            )
        grad_totals = tuple(
            (old_part + new_part for old_part, new_part in zip(grad_totals, tick_out[4]))
        )
    lifted = tuple((member[None] for member in grad_totals))
    final_parts = (
        lax.psum_scatter(lifted[0], "dp", scatter_dimension=2, tiled=True),
        lax.psum_scatter(lifted[1], "dp", scatter_dimension=1, tiled=True),
        lax.psum_scatter(lifted[2], "dp", scatter_dimension=1, tiled=True),
        lax.psum_scatter(lifted[3], "dp", scatter_dimension=1, tiled=True),
        lax.psum_scatter(lifted[4], "dp", scatter_dimension=1, tiled=True),
        lax.psum_scatter(lifted[5], "dp", scatter_dimension=2, tiled=True),
        lax.psum_scatter(lifted[6], "dp", scatter_dimension=2, tiled=True),
        lax.psum_scatter(lifted[7], "dp", scatter_dimension=1, tiled=True),
    )
    content_out = jnp.stack(
        [
            select_section(section_outputs[micro_idx][0], tick_results[micro_idx][0])
            for micro_idx in range(micro_count)
        ]
    )[None]
    query_out = jnp.stack(
        [
            select_section(section_outputs[micro_idx][1], tick_results[micro_idx][1])
            for micro_idx in range(micro_count)
        ]
    )[None]
    content_grad = jnp.stack(
        [
            select_section(tick_results[micro_idx + 1][2], tick_results[micro_idx][2])
            for micro_idx in range(micro_count)
        ]
    )[None]
    query_grad = jnp.stack(
        [
            select_section(tick_results[micro_idx + 1][3], tick_results[micro_idx][3])
            for micro_idx in range(micro_count)
        ]
    )[None]
    return (
        content_out,
        query_out,
        content_grad,
        query_grad,
        final_parts[0],
        final_parts[1],
        final_parts[2],
        final_parts[3],
        final_parts[4],
        final_parts[5],
        final_parts[6],
        final_parts[7],
    )


def solution(mesh):
    return jax.shard_map(
        body,
        mesh=mesh,
        in_specs=(
            P(None, "dp", None),
            P(None, "dp", None),
            P(None, "dp", None),
            P(None, "dp", None),
            P(None, "dp", None),
            P(None, "dp"),
            P(None, "dp"),
            P("section", None, None, None),
            P("section", None, None),
            P("section", None, None),
            P("section", None, None),
            P("section", None),
            P("section", None, None),
            P("section", None, None),
            P("section", None),
        ),
        out_specs=(
            P("section", None, "dp", None),
            P("section", None, "dp", None),
            P("section", None, "dp", None),
            P("section", None, "dp", None),
            P("section", None, "dp", None),
            P("section", "dp", None),
            P("section", "dp", None),
            P("section", "dp", None),
            P("section", "dp"),
            P("section", None, "dp"),
            P("section", None, "dp"),
            P("section", "dp"),
        ),
        check_vma=False,
    )
```

profile of v0, /device:TPU:0, one launch (start us, length us, event | category | flops | bytes accessed | tf_op | source)
XLA Modules:
  0.0 1216.3 jit_solution(6054122412525077483)
XLA Ops:
  21.5 78.4 %conditional.6 = (bf16[256,768]{1,0:T(8,128)(2,1)}, bf16[256,768]{1,0:T(8,128)(2,1)}) conditional(s32[]{:T(128)} %convert_element_type.982, () %tuple.60, (bf16[256,768]{1,0:T(8,128)(2,1)}, bf16[3,768,768]{2,1,0:T(8,128)(2,1)}, f32[6,768]{1,0:T(8,128)}, pred[256,256]{0,1:T(8,128)(4,1)}, s32[256,256]{1,0:T(8,128)}, ...), branch_computations={%region_61.62_spmd, %region_62.75_spmd} | conditional | flops 7479303680 | bytes 132344872 | solution.py:314
  51.5 13.6 %fusion.578 = (f32[256]{0:T(256)S(1)}, f32[256,768]{1,0:T(8,128)S(1)}) fusion(f32[768]{0:T(1024)} %get-tuple-element.451, bf16[3072,768]{1,0:T(8,128)(2,1)} %get-tuple-element.337, f32[3072]{0:T(1024)} %bitcast.862, bf16[768,3072]{1,0:T(8,128)(2,1)} %get-tuple-element.335, f32[256,768]{1,0:T(8,128)} %copy-done.102, f32[256]{0:T(256)S(1)} %add_rsqrt_fusion.5, ...), kind=kOutput, calls=%fused_computation.1066 | convolution fusion | flops 2470182656 | bytes 11034624 | tf_op jit(solution)/shard_map/cond/branch_1_fun/dot_general | solution.py:64
  81.6 14.1 %fusion.583 = (f32[256]{0:T(256)S(1)}, f32[256,768]{1,0:T(8,128)}) fusion(f32[768]{0:T(1024)S(1)} %copy-done.316, bf16[3072,768]{1,0:T(8,128)(2,1)} %get-tuple-element.337, f32[3072]{0:T(1024)S(1)} %bitcast.863, bf16[768,3072]{1,0:T(8,128)(2,1)} %get-tuple-element.335, f32[256,768]{1,0:T(8,128)} %copy-done.100, f32[768]{0:T(1024)S(1)} %copy-done.317, ...), kind=kOutput, calls=%fused_computation.1069 | convolution fusion | flops 2470182656 | bytes 11034624 | tf_op jit(solution)/shard_map/cond/branch_1_fun/dot_general | solution.py:64
  106.5 74.9 %conditional.4 = (bf16[256,768]{1,0:T(8,128)(2,1)}, bf16[256,768]{1,0:T(8,128)(2,1)}) conditional(s32[]{:T(128)} %convert_element_type.982, () %tuple.56, (bf16[256,768]{1,0:T(8,128)(2,1)S(1)}, bf16[3,768,768]{2,1,0:T(8,128)(2,1)}, f32[6,768]{1,0:T(8,128)}, pred[256,256]{0,1:T(8,128)(4,1)}, s32[256,256]{1,0:T(8,128)}, ...), branch_computations={%region_3.4_spmd, %region_4.17_spmd} | conditional | flops 7479303680 | bytes 129630152 | solution.py:314
  136.8 14.0 %fusion.568 = (f32[256]{0:T(256)}, f32[256,768]{1,0:T(8,128)S(1)}) fusion(f32[768]{0:T(1024)} %get-tuple-element.425, bf16[3072,768]{1,0:T(8,128)(2,1)} %get-tuple-element.306, f32[3072]{0:T(1024)} %bitcast.864, bf16[768,3072]{1,0:T(8,128)(2,1)} %get-tuple-element.304, f32[256,768]{1,0:T(8,128)S(1)} %get-tuple-element.587, f32[256]{0:T(256)} %add_rsqrt_fusion.1, ...), kind=kOutput, calls=%fused_computation.1060 | convolution fusion | flops 2470182656 | bytes 11034624 | tf_op jit(solution)/shard_map/cond/branch_1_fun/dot_general | solution.py:64
  166.5 13.3 %fusion.573 = (f32[256]{0:T(256)S(1)}, f32[256,768]{1,0:T(8,128)S(1)}) fusion(f32[768]{0:T(1024)} %get-tuple-element.425, bf16[3072,768]{1,0:T(8,128)(2,1)} %get-tuple-element.306, f32[3072]{0:T(1024)} %bitcast.865, bf16[768,3072]{1,0:T(8,128)(2,1)} %get-tuple-element.304, f32[256,768]{1,0:T(8,128)} %copy-done.101, f32[768]{0:T(1024)} %get-tuple-element.426, ...), kind=kOutput, calls=%fused_computation.1063 | convolution fusion | flops 2470182656 | bytes 11034624 | tf_op jit(solution)/shard_map/cond/branch_1_fun/dot_general | solution.py:64
  244.6 11.7 multiply_convert_fusion.10
  256.3 11.9 multiply_convert_fusion.11
  274.1 34.6 %conditional.5 = (bf16[256,768]{1,0:T(8,128)(2,1)}, bf16[256,768]{1,0:T(8,128)(2,1)}, bf16[256,768]{1,0:T(8,128)(2,1)}, bf16[256,768]{1,0:T(8,128)(2,1)}, f32[3,...) conditional(s32[]{:T(128)} %convert_element_type.991, () %tuple.58, ...), branch_computations={%region_17.18_spmd, %region_18.58_spmd} | conditional | flops 21953904640 | bytes 665860736 | solution.py:346
  314.4 74.8 %collective-permute-done.4 = bf16[256,768]{1,0:T(8,128)(2,1)S(1)} collective-permute-done((bf16[256,768]{1,0:T(8,128)(2,1)}, bf16[256,768]{1,0:T(8,128)(2,1)S(1)}, u32[]{:S(2)}, u32[]{:S(2)}) %collective-permute-start.4) | collective-permute-done | bytes 393248 | tf_op jit(solution)/shard_map/ppermute | solution.py:24
  389.2 7.6 collective-permute-done.5
  470.6 6.7 collective-permute-done.7
  477.3 161.1 %conditional.7 = (bf16[256,768]{1,0:T(8,128)(2,1)}, bf16[256,768]{1,0:T(8,128)(2,1)}, f32[3,768,768]{2,1,0:T(8,128)}, f32[768,768]{1,0:T(8,128)}, f32[768,3072]{...) conditional(s32[]{:T(128)} %convert_element_type.982, () %tuple.62, ...), branch_computations={%region_97.98_spmd, %region_98.138_spmd} | conditional | flops 21951154176 | bytes 598066496 | solution.py:346
  522.1 10.7 multiply_convert_fusion.5
  532.8 8.1 multiply_convert_fusion.7
  658.7 8.4 fusion.435
  673.0 12.3 %add_bitcast_fusion.3 = f32[1,768,3072]{2,1,0:T(8,128)} fusion(f32[768,3072]{1,0:T(8,128)} %get-tuple-element.413, f32[768,3072]{1,0:T(8,128)} %get-tuple-element.412, f32[768,3072]{1,0:T(8,128)S(1)} %fusion.545, f32[768,3072]{1,0:T(8,128)S(1)} %fusion.542), kind=kLoop, calls=%fused_computation.748 | loop fusion | flops 7077888 | bytes 47185920 | tf_op jit(solution)/shard_map/broadcast_in_dim | solution.py:361
  690.6 11.5 add_bitcast_fusion.2
  722.5 31.2 %all-reduce = f32[1,384]{1,0:T(1,128)S(1)} all-reduce(f32[1,384]{1,0:T(1,128)S(1)} %broadcast_in_dim.473), channel_id=9, replica_groups=mesh['section'=2,'dp'=16] {'dp'}, use_global_device_ids=true, to_apply=%region_162.163.clone | all-reduce | flops 384 | bytes 3072
  761.2 56.0 %reduce-scatter.25.cloned.1.call-done = f32[48,6]{1,0:T(8,128)} async-done(((f32[768,6]{1,0:T(8,128)}), f32[48,6]{1,0:T(8,128)}) %reduce-scatter.25.cloned.1.call-update) | async-done | bytes 1168
  818.7 65.2 %reduce-scatter.17.cloned.1.call-done = f32[1,48,768]{2,1,0:T(8,128)} async-done(((f32[1,768,768]{2,1,0:T(8,128)}), f32[1,48,768]{2,1,0:T(8,128)}) %reduce-scatter.17.cloned.1.call-update) | async-done | bytes 147472 | tf_op jit(solution)/shard_map/reduce_scatter | solution.py:364
  883.9 93.5 %reduce-scatter.15.cloned.1.call-done = f32[1,3,48,768]{3,2,1,0:T(8,128)} async-done(((f32[1,3,768,768]{3,2,1,0:T(8,128)}), f32[1,3,48,768]{3,2,1,0:T(8,128)}) %reduce-scatter.15.cloned.1.call-update) | async-done | bytes 442384 | tf_op jit(solution)/shard_map/reduce_scatter | solution.py:363
  977.4 116.0 %reduce-scatter.19.cloned.1.call-done = f32[1,48,3072]{2,1,0:T(8,128)} async-done(((f32[1,768,3072]{2,1,0:T(8,128)}), f32[1,48,3072]{2,1,0:T(8,128)}) %reduce-scatter.19.cloned.1.call-update) | async-done | bytes 589840 | tf_op jit(solution)/shard_map/reduce_scatter | solution.py:365
  1093.4 115.8 %reduce-scatter.21.cloned.1.call-done = f32[1,192,768]{2,1,0:T(8,128)} async-done(((f32[1,3072,768]{2,1,0:T(8,128)}), f32[1,192,768]{2,1,0:T(8,128)}) %reduce-scatter.21.cloned.1.call-update) | async-done | bytes 589840 | tf_op jit(solution)/shard_map/reduce_scatter | solution.py:366
  (923 shorter events, 485.2 us)
Async XLA Ops:
  7.2 751.1 %reduce-scatter.27.cloned.1.call-start = ((), (), s32[]{:S(2)}) async-start(), calls=%async_computation.13 | async-start | bytes 417792
  18.1 88.4 %copy-start.73 = (bf16[256,768]{1,0:T(8,128)(2,1)}, bf16[256,768]{1,0:T(8,128)(2,1)S(1)}, u32[]{:S(2)}) copy-start(bf16[256,768]{1,0:T(8,128)(2,1)S(1)} %get-tuple-element.691) | copy-start | bytes 1179652
  99.9 106.7 %collective-permute-start.2 = (bf16[256,768]{1,0:T(8,128)(2,1)}, bf16[256,768]{1,0:T(8,128)(2,1)}, u32[]{:S(2)}, u32[]{:S(2)}) collective-permute-start(bf16[256,768]{1,0:T(8,128)(2,1)} %get-tuple-element.401), channel_id=1, source_target_pairs={{0,16},{1,17},{2,18},{3,19},{4,20},{5,21},{6,22},{7,23},{8,24},{9,... | collective-permute-start | bytes 1179656 | tf_op jit(solution)/shard_map/ppermute | solution.py:24
  101.9 113.6 %collective-permute-start.3 = (bf16[256,768]{1,0:T(8,128)(2,1)}, bf16[256,768]{1,0:T(8,128)(2,1)}, u32[]{:S(2)}, u32[]{:S(2)}) collective-permute-start(bf16[256,768]{1,0:T(8,128)(2,1)} %get-tuple-element.403), channel_id=1, source_target_pairs={{0,16},{1,17},{2,18},{3,19},{4,20},{5,21},{6,22},{7,23},{8,24},{9,... | collective-permute-start | bytes 1179656 | tf_op jit(solution)/shard_map/ppermute | solution.py:24
  181.5 92.6 %collective-permute-start = (bf16[256,768]{1,0:T(8,128)(2,1)}, bf16[256,768]{1,0:T(8,128)(2,1)}, u32[]{:S(2)}, u32[]{:S(2)}) collective-permute-start(bf16[256,768]{1,0:T(8,128)(2,1)} %get-tuple-element.398), channel_id=1, source_target_pairs={{0,16},{1,17},{2,18},{3,19},{4,20},{5,21},{6,22},{7,23},{8,24},{9,... | collective-permute-start | bytes 1179656 | tf_op jit(solution)/shard_map/ppermute | solution.py:24
  183.5 90.6 %collective-permute-start.1 = (bf16[256,768]{1,0:T(8,128)(2,1)}, bf16[256,768]{1,0:T(8,128)(2,1)}, u32[]{:S(2)}, u32[]{:S(2)}) collective-permute-start(bf16[256,768]{1,0:T(8,128)(2,1)} %get-tuple-element.399), channel_id=1, source_target_pairs={{0,16},{1,17},{2,18},{3,19},{4,20},{5,21},{6,22},{7,23},{8,24},{9,... | collective-permute-start | bytes 1179656 | tf_op jit(solution)/shard_map/ppermute | solution.py:24
  308.7 91.2 %copy-start.19 = (f32[256,768]{1,0:T(8,128)S(1)}, f32[256,768]{1,0:T(8,128)}, u32[]{:S(2)}) copy-start(f32[256,768]{1,0:T(8,128)} %get-tuple-element.736) | copy-start | bytes 2359300
  308.7 91.2 %copy-start.21 = (f32[256,768]{1,0:T(8,128)S(1)}, f32[256,768]{1,0:T(8,128)}, u32[]{:S(2)}) copy-start(f32[256,768]{1,0:T(8,128)} %get-tuple-element.743) | copy-start | bytes 2359300
  308.7 91.2 %copy-start.202 = (f32[768]{0:T(1024)S(1)}, f32[768]{0:T(1024)}, u32[]{:S(2)}) copy-start(f32[768]{0:T(1024)} %get-tuple-element.495) | copy-start | bytes 9220
  308.7 91.2 %copy-start.214 = (f32[256]{0:T(256)S(1)}, f32[256]{0:T(256)}, u32[]{:S(2)}) copy-start(f32[256]{0:T(256)} %broadcast_multiply_fusion.18) | copy-start | bytes 3076
  308.8 91.2 %copy-start.216 = (f32[256]{0:T(256)S(1)}, f32[256]{0:T(256)}, u32[]{:S(2)}) copy-start(f32[256]{0:T(256)} %broadcast_multiply_fusion.16) | copy-start | bytes 3076
  308.8 80.5 %collective-permute-start.4 = (bf16[256,768]{1,0:T(8,128)(2,1)}, bf16[256,768]{1,0:T(8,128)(2,1)S(1)}, u32[]{:S(2)}, u32[]{:S(2)}) collective-permute-start(bf16[256,768]{1,0:T(8,128)(2,1)} %get-tuple-element.404), channel_id=1, source_target_pairs={{16,0},{17,1},{18,2},{19,3},{20,4},{21,5},{22,6},{23,7},{24,8},{25... | collective-permute-start | bytes 1179656 | tf_op jit(solution)/shard_map/ppermute | solution.py:24
  310.2 86.7 %collective-permute-start.5 = (bf16[256,768]{1,0:T(8,128)(2,1)}, bf16[256,768]{1,0:T(8,128)(2,1)S(1)}, u32[]{:S(2)}, u32[]{:S(2)}) collective-permute-start(bf16[256,768]{1,0:T(8,128)(2,1)} %get-tuple-element.405), channel_id=1, source_target_pairs={{16,0},{17,1},{18,2},{19,3},{20,4},{21,5},{22,6},{23,7},{24,8},{25... | collective-permute-start | bytes 1179656 | tf_op jit(solution)/shard_map/ppermute | solution.py:24
  311.5 89.3 %slice-start.8 = ((s8[4718592]{0:T(1024)(128)(4,1)}), s8[4194304]{0:T(1024)(128)(4,1)S(1)}, s32[]{:S(2)}) async-start(s8[4718592]{0:T(1024)(128)(4,1)} %bitcast.852), calls=%async_computation.22 | async-start | bytes 8388608
  314.4 86.2 %copy-start.265 = (f32[256]{0:T(256)}, f32[256]{0:T(256)S(1)}, u32[]{:S(2)}) copy-start(f32[256]{0:T(256)S(1)} %get-tuple-element.761) | copy-start | bytes 3076
  314.4 86.2 %copy-start.267 = (f32[256]{0:T(256)}, f32[256]{0:T(256)S(1)}, u32[]{:S(2)}) copy-start(f32[256]{0:T(256)S(1)} %get-tuple-element.762) | copy-start | bytes 3076
  456.4 14.2 %collective-permute-start.6 = (bf16[256,768]{1,0:T(8,128)(2,1)S(1)}, bf16[256,768]{1,0:T(8,128)(2,1)}, u32[]{:S(2)}, u32[]{:S(2)}) collective-permute-start(bf16[256,768]{1,0:T(8,128)(2,1)S(1)} %fusion.456), channel_id=1, source_target_pairs={{16,0},{17,1},{18,2},{19,3},{20,4},{21,5},{22,6},{23,7},{24,8},{25... | collective-permute-start | bytes 1179656 | tf_op jit(solution)/shard_map/ppermute | solution.py:24
  459.7 17.6 %collective-permute-start.7 = (bf16[256,768]{1,0:T(8,128)(2,1)S(1)}, bf16[256,768]{1,0:T(8,128)(2,1)}, u32[]{:S(2)}, u32[]{:S(2)}) collective-permute-start(bf16[256,768]{1,0:T(8,128)(2,1)S(1)} %fusion.457), channel_id=1, source_target_pairs={{16,0},{17,1},{18,2},{19,3},{20,4},{21,5},{22,6},{23,7},{24,8},{25... | collective-permute-start | bytes 1179656 | tf_op jit(solution)/shard_map/ppermute | solution.py:24
  640.7 118.9 %reduce-scatter.23.cloned.1.call-start = ((), (), s32[]{:S(2)}) async-start(), calls=%async_computation.11 | async-start | bytes 1671168
  646.3 170.9 %reduce-scatter.25.cloned.1.call-start = ((), (), s32[]{:S(2)}) async-start(), calls=%async_computation.12 | async-start | bytes 417792
  650.1 233.8 %reduce-scatter.17.cloned.1.call-start = ((), (), s32[]{:S(2)}) async-start(), calls=%async_computation.8 | async-start | bytes 2506752 | tf_op jit(solution)/shard_map/reduce_scatter | solution.py:364
  655.5 321.9 %reduce-scatter.15.cloned.1.call-start = ((), (), s32[]{:S(2)}) async-start(), calls=%async_computation.7 | async-start | bytes 7520256 | tf_op jit(solution)/shard_map/reduce_scatter | solution.py:363
  667.3 426.1 %reduce-scatter.19.cloned.1.call-start = ((), (), s32[]{:S(2)}) async-start(), calls=%async_computation.9 | async-start | bytes 10027008 | tf_op jit(solution)/shard_map/reduce_scatter | solution.py:365
  685.3 523.8 %reduce-scatter.21.cloned.1.call-start = ((), (), s32[]{:S(2)}) async-start(), calls=%async_computation.10 | async-start | bytes 10027008 | tf_op jit(solution)/shard_map/reduce_scatter | solution.py:366
  (258 other events, 1887.9 us)
Sparse Core Ops, SparseCore 0:
  640.9 55.4 reduce-scatter.26
  700.5 58.5 reduce-scatter.22
  762.5 54.5 reduce-scatter.24
  821.8 62.0 reduce-scatter.16
  888.3 89.0 reduce-scatter.14
  982.5 110.8 reduce-scatter.18
  1098.0 111.0 reduce-scatter.20
where the time goes:
time: 1220 us
  waiting for transfers between devices  539 us (44%)
  matrix products  334 us (27%)
  local copies, waits for them, and re-layouts  140 us (11%)
  other arithmetic  123 us (10%)
  blocking collectives  31.2 us (3%)
  loops' own time  17.7 us (1%)
  between operations  16.9 us (1%)
  starting transfers between devices  14.3 us (1%)
    dot_general x36, matrix products, matmul(): return jnp.dot(left, right, preferred_element_type=jnp.float32)  147 us
    reduce_scatter x1, waiting for transfers between devices, body(): lax.psum_scatter(lifted[2], 'dp', scatter_dimension=1, tiled=True)  116 us
    reduce_scatter x1, waiting for transfers between devices, body(): lax.psum_scatter(lifted[3], 'dp', scatter_dimension=1, tiled=True)  116 us
    reduce_scatter x1, waiting for transfers between devices, body(): lax.psum_scatter(lifted[0], 'dp', scatter_dimension=2, tiled=True)  93.5 us
    ppermute x8, waiting for transfers between devices, from_behind(): return lax.ppermute(block, axis, route)  92.6 us
    reduce_scatter x1, waiting for transfers between devices, body(): lax.psum_scatter(lifted[1], 'dp', scatter_dimension=1, tiled=True)  65.2 us
    unnamed x10, waiting for transfers between devices  56.1 us
    dot_general x20, matrix products, times_transpose(): jnp.einsum('ra,ba->rb', left, right, preferred_element_type=jnp.float32)  39.3 us
  transfers between devices with their start and end apart: 15, of which 9 were waited for; matrix products, arithmetic and copies ran while one was open for 21% of the time, Pallas kernels for 0%

commit v1 on v0

v1 whole, which is shorter than its diff:
```python
from functools import partial

import jax
import jax.numpy as jnp
from jax import lax
from jax.experimental import pallas as pl
from jax.experimental.pallas import tpu as pltpu
from jax.sharding import PartitionSpec as P

LN_EPS = 1e-05
NEG_FILL = -1e30
BUCKET_EDGES = (12, 16, 23, 32, 46, 64, 91)
BUCKETS = 32
F32, BF16 = jnp.float32, jnp.bfloat16
VMEM_LIMIT = 60 * 1024 * 1024
TAIL = (0.127414796, -0.142248368, 0.7107068705, -0.7265760135, 0.5307027145)
TAIL_SLOPE = 0.3275911 / 2**0.5
DENSITY = 0.3989422804014327


def nn(left, right):
    return jnp.dot(left, right, preferred_element_type=F32)


def nt(left, right):
    return lax.dot_general(left, right, (((1,), (1,)), ((), ())), preferred_element_type=F32)


def iota(shape, dim):
    return lax.broadcasted_iota(jnp.int32, shape, dim)


def bucket_index(relative):
    magnitude = jnp.abs(relative)
    far_part = jnp.full_like(magnitude, 8)
    for edge_at in BUCKET_EDGES:
        far_part = far_part + jnp.where(magnitude >= edge_at, 1, 0)
    near_far = jnp.where(magnitude < 8, magnitude, far_part)
    return near_far + jnp.where(relative > 0, 16, 0)


def gelu_and_slope(v):
    z = jnp.abs(v)
    t = 1.0 / (1.0 + TAIL_SLOPE * z)
    poly = TAIL[4]
    for coefficient in TAIL[3::-1]:
        poly = coefficient + t * poly
    bell = jnp.exp(-0.5 * (v * v))
    tail = t * poly * bell
    below = jnp.where(v >= 0, 1.0 - tail, tail)
    return v * below, below + DENSITY * (v * bell)


class Copies:
    def __init__(self, sems):
        self.sems, self.used, self.open = sems, 0, []

    def start(self, src, dst):
        copy = pltpu.make_async_copy(src, dst, self.sems.at[self.used])
        self.used += 1
        copy.start()
        return copy

    def out(self, src, dst):
        self.open.append(self.start(src, dst))

    def finish(self):
        for copy in self.open:
            copy.wait()


def head_map(entries, heads, span):
    entry = iota((16, entries), 1)
    own_head = (entry - heads * ((entry * 5462) >> 16)) == iota((16, entries), 0)
    bucket = bucket_index(span // 2 - iota((entries, span), 1))
    row = iota((entries, span), 0)
    own_bucket = (row >= heads * bucket) & (row < heads * bucket + heads)
    return own_head, own_bucket


def make_masks(lengths, order_ref, predicted_ref, m, rows):
    def place(shape, dim):
        token = iota(shape, dim)
        segment, start, end = jnp.zeros(shape, jnp.int32), jnp.zeros(shape, jnp.int32), 0
        for slot in range(lengths.shape[2]):
            size = lengths[m, 0, slot]
            end = end + size
            passed = token >= end
            segment = segment + jnp.where(passed, 1, 0)
            start = start + jnp.where(passed, size, 0)
        inside = token < end
        return jnp.where(inside, segment, -1 - token), inside & (token - start > 0)

    segment, later = place((1, rows), 1)
    order = order_ref[pl.ds(m, 1), :]
    flag = (predicted_ref[pl.ds(m, 1), :] > 0) & later
    gate = jnp.where(flag, order, -1).astype(F32)
    gate_column = jnp.transpose(jnp.broadcast_to(gate, (128, rows)))
    segment_column = jnp.transpose(jnp.broadcast_to(segment.astype(F32), (128, rows)))
    gate_column = jnp.concatenate([gate_column] * (rows // 128), axis=1)
    segment_column = jnp.concatenate([segment_column] * (rows // 128), axis=1)
    same = segment_column == segment.astype(F32)
    order = order.astype(F32)
    return [
        jnp.where(same & (gate_column <= order), 0.0, NEG_FILL),
        jnp.where(same & (gate_column < order), 0.0, NEG_FILL),
    ]


def fwd_kernel(m, names_in, names_out, *refs):
    r = dict(zip(names_in, refs))
    refs = refs[len(names_in):]
    r.update(zip(names_out, refs))
    (x_s, wp_s, wo_s, wu_s, wd_s, q_t, k_s, k_t, v_s, v_t, mask_s, toep_s, e_s, inv_s, mix_t, mix_s,
     sum_s, nl_s, act_s, gp_s, xh_s, rs_s, out_s, sems) = refs[len(names_out):]
    rows = x_s.shape[0] // 2
    width = x_s.shape[1]
    heads = r["rel_table"].shape[1] // BUCKETS
    depth = width // heads
    hidden = wu_s.shape[1]
    span = 2 * rows

    @pl.when(r["active"][0] == 1)
    def _():
        cp = Copies(sems)
        if r["xc"].shape[0] == rows:
            xc, xq = r["xc"], r["xq"]
        else:
            xc, xq = r["xc"].at[pl.ds(m * rows, rows)], r["xq"].at[pl.ds(m * rows, rows)]
        get_x = [cp.start(xc, x_s.at[pl.ds(0, rows)]), cp.start(xq, x_s.at[pl.ds(rows, rows)])]
        get_p = [cp.start(r["proj_weight"].at[0, i], wp_s.at[i]) for i in range(3)]
        get_o = cp.start(r["out_weight"].at[0], wo_s)
        get_u = cp.start(r["up_weight"].at[0], wu_s)
        get_d = cp.start(r["down_weight"].at[0], wd_s)

        masks = make_masks(r["lengths"], r["order"], r["predicted"], m, rows)
        mask_s[0], mask_s[1] = masks
        own_head, own_bucket = head_map(heads * BUCKETS, heads, span)
        picked = jnp.where(own_head, r["rel_table"][...], 0.0)
        toep_s[...] = jnp.dot(
            picked, jnp.where(own_bucket, 1.0, 0.0), precision=lax.Precision.HIGHEST, preferred_element_type=F32
        )
        biases = r["biases"]
        gains = r["gains"]

        for copy in get_x:
            copy.wait()
        wrows = [pl.ds(s * 2 * rows + m * rows, rows) for s in range(2)]
        for s in range(2):
            cp.out(x_s.at[pl.ds(s * rows, rows)], r["w_x"].at[wrows[s]])
        step = 256
        get_p[0].wait()
        for n in range(0, width, step):
            q = nn(x_s[...], wp_s[0, :, n:n + step]) + biases[0, 0:1, n:n + step]
            q_t[n:n + step, :] = jnp.transpose(q.astype(BF16) * 0.125)
        get_p[1].wait()
        get_p[2].wait()
        for n in range(0, width, step):
            k = nn(x_s[0:rows, :], wp_s[1, :, n:n + step]).astype(BF16)
            k_s[:, n:n + step] = k
            k_t[n:n + step, :] = jnp.transpose(k)
            v = (nn(x_s[0:rows, :], wp_s[2, :, n:n + step]) + biases[0, 1:2, n:n + step]).astype(BF16)
            v_s[:, n:n + step] = v
            v_t[n:n + step, :] = jnp.transpose(v)
        cp.out(q_t, r["q_t"])
        cp.out(k_s, r["k"])
        cp.out(k_t, r["k_t"])
        cp.out(v_s, r["v"])

        blank = jnp.zeros((depth, 2 * rows), BF16)

        def pair_step(pair, carry):
            base = pl.multiple_of(pair * 2 * depth, 2 * depth)
            k_pair = k_s[:, pl.ds(base, 2 * depth)]
            for half in range(2):
                head = 2 * pair + half
                at = pl.multiple_of(base + half * depth, depth)
                q_head = q_t[pl.ds(at, depth), :]
                stacked = jnp.concatenate([q_head, blank] if half == 0 else [blank, q_head], axis=0)
                scores = nn(k_pair, stacked)
                line = jnp.broadcast_to(toep_s[pl.ds(head, 1), :], (rows, span))
                rel = pltpu.roll(line, rows, 1, stride=1, stride_axis=0)[:, :rows]
                for s in range(2):
                    logits = scores[:, s * rows:(s + 1) * rows] + rel + mask_s[s]
                    top = jnp.max(logits, axis=0, keepdims=True)
                    e = jnp.exp(logits - top)
                    inv = 1.0 / jnp.sum(e, axis=0, keepdims=True)
                    e = e.astype(BF16)
                    e_s[s, head] = e
                    inv_s[s, pl.ds(head, 1), :] = inv
                    mixed = nn(v_t[pl.ds(at, depth), :], e) * inv
                    mix_t[pl.ds(at, depth), s * rows:(s + 1) * rows] = mixed.astype(BF16)
            return carry

        lax.fori_loop(0, heads // 2, pair_step, 0)
        cp.out(e_s, r["e"])
        cp.out(inv_s, r["inv"])
        for s in range(2):
            cp.out(mix_t.at[:, pl.ds(s * rows, rows)], r["w_mix_t"].at[:, wrows[s]])
        for n in range(0, width, step):
            mix_s[:, n:n + step] = jnp.transpose(mix_t[n:n + step, :])
        get_o.wait()
        for n in range(0, width, step):
            sum_s[:, n:n + step] = nn(mix_s[...], wo_s[:, n:n + step])

        block = 64

        def norm_one(i, carry):
            at = pl.ds(pl.multiple_of(i * block, block), block)
            summed = x_s[at, :].astype(F32) + sum_s[at, :] + biases[0, 2:3, :]
            center = summed - jnp.mean(summed, axis=1, keepdims=True)
            scale = lax.rsqrt(jnp.mean(center * center, axis=1, keepdims=True) + LN_EPS)
            xhat = center * scale
            normed = xhat * gains[0, 0:1, :] + biases[0, 4:5, :]
            xh_s[0, at, :] = xhat.astype(BF16)
            rs_s[0, at, :] = jnp.broadcast_to(scale, (block, 128))
            nl_s[at, :] = normed.astype(BF16)
            sum_s[at, :] = normed + biases[0, 3:4, :]
            return carry

        lax.fori_loop(0, 2 * rows // block, norm_one, 0)
        for s in range(2):
            cp.out(nl_s.at[pl.ds(s * rows, rows)], r["w_nl"].at[wrows[s]])
        get_u.wait()
        chunk = 512

        def up_step(j, carry):
            at = pl.ds(pl.multiple_of(j * chunk, chunk), chunk)
            pre = nn(nl_s[...], wu_s[:, at]) + r["up_bias"][0:1, at]
            act, slope = gelu_and_slope(pre)
            act_s[:, at] = act.astype(BF16)
            gp_s[:, at] = slope.astype(BF16)
            return carry

        lax.fori_loop(0, hidden // chunk, up_step, 0)
        cp.out(gp_s, r["gp"])
        for s in range(2):
            cp.out(act_s.at[pl.ds(s * rows, rows)], r["w_act"].at[wrows[s]])
        get_d.wait()
        for n in range(0, width, step):
            sum_s[:, n:n + step] += nn(act_s[...], wd_s[:, n:n + step])

        def norm_two(i, carry):
            at = pl.ds(pl.multiple_of(i * block, block), block)
            total = sum_s[at, :]
            center = total - jnp.mean(total, axis=1, keepdims=True)
            scale = lax.rsqrt(jnp.mean(center * center, axis=1, keepdims=True) + LN_EPS)
            xhat = center * scale
            xh_s[1, at, :] = xhat.astype(BF16)
            rs_s[1, at, :] = jnp.broadcast_to(scale, (block, 128))
            out_s[at, :] = (xhat * gains[0, 1:2, :] + biases[0, 5:6, :]).astype(BF16)
            return carry

        lax.fori_loop(0, 2 * rows // block, norm_two, 0)
        for s in range(2):
            cp.out(out_s.at[pl.ds(s * rows, rows)], r["out"].at[s])
        cp.out(xh_s, r["xhat"])
        cp.out(rs_s, r["scale"])
        cp.finish()


def bwd_kernel(m, names_in, names_out, *refs):
    r = dict(zip(names_in, refs))
    refs = refs[len(names_in):]
    r.update(zip(names_out, refs))
    (g_s, wp_s, wo_s, wu_s, wd_s, q_t, k_s, k_t, v_s, e_s, inv_s, gp_s, xh_s, rs_s,
     grad_s, dz_s, dpre_s, acc_s, da_s, dm_t, dq_t, dk_t, dv_t, dq_s, dk_s, dv_s, diag_s, small_s, upb_s, tab_s,
     out_s, sems) = refs[len(names_out):]
    rows = g_s.shape[0] // 2
    width = g_s.shape[1]
    heads = r["rel_table"].shape[1] // BUCKETS
    depth = width // heads
    hidden = wu_s.shape[1]
    span = 2 * rows

    @pl.when(r["active"][0] == 1)
    def _():
        cp = Copies(sems)
        if r["gc"].shape[0] == rows:
            gc, gq = r["gc"], r["gq"]
        else:
            gc, gq = r["gc"].at[pl.ds(m * rows, rows)], r["gq"].at[pl.ds(m * rows, rows)]
        wrows = [pl.ds(s * 2 * rows + m * rows, rows) for s in range(2)]
        get_g = [cp.start(gc, g_s.at[pl.ds(0, rows)]), cp.start(gq, g_s.at[pl.ds(rows, rows)])]
        get_g += [cp.start(r["xhat"], xh_s), cp.start(r["scale"], rs_s)]
        get_d = cp.start(r["down_weight"].at[0], wd_s)
        get_gp = cp.start(r["gp"], gp_s)
        get_u = cp.start(r["up_weight"].at[0], wu_s)
        get_o = cp.start(r["out_weight"].at[0], wo_s)
        get_a = [cp.start(r["inv"], inv_s)]
        get_e = [cp.start(r["e"], e_s), cp.start(r["q_t"], q_t), cp.start(r["k"], k_s)]
        get_e += [cp.start(r["k_t"], k_t), cp.start(r["v"], v_s)]
        get_p = [cp.start(r["proj_weight"].at[0, i], wp_s.at[i]) for i in range(3)]
        gains = r["gains"]
        small_s[...] = jnp.zeros(small_s.shape, F32)
        step, block, chunk = 256, 64, 512

        def add_small(row, value):
            small_s[row:row + 1, :] += jnp.sum(value, axis=0, keepdims=True)

        for copy in get_g:
            copy.wait()

        def norm_two(i, carry):
            at = pl.ds(pl.multiple_of(i * block, block), block)
            grad = g_s[at, :].astype(F32)
            xhat = xh_s[1, at, :].astype(F32)
            both = grad * xhat
            add_small(7, both)
            add_small(5, grad)
            scaled = grad * gains[0, 1:2, :]
            mean_a = jnp.mean(scaled, axis=1, keepdims=True)
            mean_b = jnp.mean(scaled * xhat, axis=1, keepdims=True)
            back = (scaled - mean_a - xhat * mean_b) * rs_s[1, at, 0:1]
            grad_s[at, :] = back
            low = back.astype(BF16)
            dz_s[at, :] = low
            add_small(3, low.astype(F32))
            return carry

        lax.fori_loop(0, 2 * rows // block, norm_two, 0)
        for s in range(2):
            cp.out(dz_s.at[pl.ds(s * rows, rows)], r["w_dz"].at[wrows[s]])
        get_d.wait()
        get_gp.wait()

        def up_step(j, carry):
            at = pl.ds(pl.multiple_of(j * chunk, chunk), chunk)
            d_act = nt(dz_s[...], wd_s[at, :])
            d_pre = (d_act * gp_s[:, at].astype(F32)).astype(BF16)
            dpre_s[:, at] = d_pre
            upb_s[0:1, at] = jnp.sum(d_pre.astype(F32), axis=0, keepdims=True)
            return carry

        lax.fori_loop(0, hidden // chunk, up_step, 0)
        for s in range(2):
            cp.out(dpre_s.at[pl.ds(s * rows, rows)], r["w_dpre"].at[wrows[s]])
        get_u.wait()
        for n in range(0, width, step):
            acc_s[:, n:n + step] = nt(dpre_s[...], wu_s[n:n + step, :])

        def norm_one(i, carry):
            at = pl.ds(pl.multiple_of(i * block, block), block)
            grad = grad_s[at, :] + acc_s[at, :]
            xhat = xh_s[0, at, :].astype(F32)
            add_small(6, grad * xhat)
            add_small(4, grad)
            scaled = grad * gains[0, 0:1, :]
            mean_a = jnp.mean(scaled, axis=1, keepdims=True)
            mean_b = jnp.mean(scaled * xhat, axis=1, keepdims=True)
            back = (scaled - mean_a - xhat * mean_b) * rs_s[0, at, 0:1]
            grad_s[at, :] = back
            low = back.astype(BF16)
            da_s[at, :] = low
            add_small(2, low.astype(F32))
            return carry

        lax.fori_loop(0, 2 * rows // block, norm_one, 0)
        for s in range(2):
            cp.out(da_s.at[pl.ds(s * rows, rows)], r["w_da"].at[wrows[s]])
        get_o.wait()
        for copy in get_a:
            copy.wait()
        for n in range(0, width, step):
            d_mix = nt(wo_s[n:n + step, :], da_s[...])
            for h in range(n // depth, (n + step) // depth):
                part = d_mix[h * depth - n:(h + 1) * depth - n, :]
                inv = jnp.concatenate([inv_s[s, h:h + 1, :] for s in range(2)], axis=1)
                dm_t[h * depth:(h + 1) * depth, :] = (part * inv).astype(BF16)
        for copy in get_e:
            copy.wait()
        blank = jnp.zeros((depth, 2 * rows), BF16)
        diag_s[...] = jnp.zeros(diag_s.shape, F32)

        def pair_step(pair, carry):
            base = pl.multiple_of(pair * 2 * depth, 2 * depth)
            v_pair = v_s[:, pl.ds(base, 2 * depth)]
            for half in range(2):
                head = 2 * pair + half
                at = pl.ds(pl.multiple_of(base + half * depth, depth), depth)
                dm_head = dm_t[at, :]
                stacked = jnp.concatenate([dm_head, blank] if half == 0 else [blank, dm_head], axis=0)
                d_prob = nn(v_pair, stacked)
                parts, whole = [], 0.0
                for s in range(2):
                    e = e_s[s, head].astype(F32)
                    part = d_prob[:, s * rows:(s + 1) * rows]
                    mean = jnp.sum(e * part, axis=0, keepdims=True) * inv_s[s, pl.ds(head, 1), :]
                    d_score = (e * (part - mean)).astype(BF16)
                    parts.append(d_score)
                    whole = whole + d_score.astype(F32)
                both = jnp.concatenate(parts, axis=1)
                e_both = jnp.concatenate([e_s[0, head], e_s[1, head]], axis=1)
                dq_t[at, :] = (nn(k_t[at, :], both) * 0.125).astype(BF16)
                dv_t[at, :] = nt(dm_head, e_both).astype(BF16)
                dk_t[at, :] = nt(q_t[at, :], both).astype(BF16)
                wide = jnp.concatenate([jnp.zeros_like(whole), whole], axis=1)
                count = rows
                while count > 8:
                    count //= 2
                    wide = wide[:count, :] + pltpu.roll(wide[count:, :], span - count, 1)
                line = wide[0:1, :]
                for k in range(1, 8):
                    line = line + pltpu.roll(wide, span - k, 1)[k:k + 1, :]
                diag_s[pl.ds(head, 1), :] = line
            return carry

        lax.fori_loop(0, heads // 2, pair_step, 0)
        for n in range(0, width, step):
            part = jnp.transpose(dq_t[n:n + step, :])
            dq_s[:, n:n + step] = part
            small_s[0:1, n:n + step] = jnp.sum(part.astype(F32), axis=0, keepdims=True)
            dk_s[:, n:n + step] = jnp.transpose(dk_t[n:n + step, :])
            part = jnp.transpose(dv_t[n:n + step, :])
            dv_s[:, n:n + step] = part
            small_s[1:2, n:n + step] = jnp.sum(part.astype(F32), axis=0, keepdims=True)
        for s in range(2):
            cp.out(dq_s.at[pl.ds(s * rows, rows)], r["w_dq"].at[wrows[s]])
        cp.out(dk_s, r["w_dk"].at[pl.ds(m * rows, rows)])
        cp.out(dv_s, r["w_dv"].at[pl.ds(m * rows, rows)])
        for copy in get_p:
            copy.wait()
        for n in range(0, width, step):
            back = grad_s[:, n:n + step] + nt(dq_s[...], wp_s[0, n:n + step, :])
            more = nt(dk_s[...], wp_s[1, n:n + step, :]) + nt(dv_s[...], wp_s[2, n:n + step, :])
            out_s[0:rows, n:n + step] = (back[0:rows, :] + more).astype(BF16)
            out_s[rows:, n:n + step] = back[rows:, :].astype(BF16)
        for s in range(2):
            cp.out(out_s.at[pl.ds(s * rows, rows)], r["grad"].at[s])

        own_head, own_bucket = head_map(heads * BUCKETS, heads, span)
        folded = lax.dot_general(
            diag_s[...],
            jnp.where(own_bucket, 1.0, 0.0),
            (((1,), (1,)), ((), ())),
            precision=lax.Precision.HIGHEST,
            preferred_element_type=F32,
        )
        tab_s[...] = jnp.broadcast_to(
            jnp.sum(jnp.where(own_head, folded, 0.0), axis=0, keepdims=True), tab_s.shape
        )
        cp.out(small_s, r["small"])
        cp.out(upb_s, r["up_small"])
        cp.out(tab_s, r["tab_small"])
        cp.finish()


SMEM = pl.BlockSpec(memory_space=pltpu.SMEM)
VMEM = pl.BlockSpec(memory_space=pltpu.VMEM)
ANY = pl.BlockSpec(memory_space=pl.ANY)


def call(kernel, m, operands, buffers, made, scratch, flops, copies):
    names_in = list(operands) + ["old_" + name for name in buffers]
    names_out = list(buffers) + list(made)
    shapes = [jax.ShapeDtypeStruct(a.shape, a.dtype) for a in buffers.values()] + list(made.values())
    outs = pl.pallas_call(
        partial(kernel, m, names_in, names_out),
        in_specs=[spec for _, spec in operands.values()] + [ANY] * len(buffers),
        out_specs=[ANY] * len(names_out),
        out_shape=shapes,
        scratch_shapes=scratch + [pltpu.SemaphoreType.DMA((copies,))],
        input_output_aliases={len(operands) + i: i for i in range(len(buffers))},
        compiler_params=pltpu.CompilerParams(vmem_limit_bytes=VMEM_LIMIT),
        cost_estimate=pl.CostEstimate(flops=flops, bytes_accessed=30_000_000, transcendentals=0),
    )(*[a for a, _ in operands.values()], *buffers.values())
    return dict(zip(names_out, outs))


def shape(*dims, dtype=BF16):
    return jax.ShapeDtypeStruct(dims, dtype)


def forward_shapes(rows, width, hidden, heads):
    return {
        "q_t": shape(width, 2 * rows),
        "k": shape(rows, width),
        "k_t": shape(width, rows),
        "v": shape(rows, width),
        "e": shape(2, heads, rows, rows),
        "inv": shape(2, 16, rows, dtype=F32),
        "gp": shape(2 * rows, hidden),
        "xhat": shape(2, 2 * rows, width),
        "scale": shape(2, 2 * rows, 128, dtype=F32),
        "out": shape(2, rows, width),
    }


def forward(m, active, xc, xq, fixed, weights, kept, store):
    rows, width, hidden, heads, micro = fixed["dims"]
    operands = {
        "active": (active, SMEM),
        "lengths": (fixed["lengths"], SMEM),
        "order": (fixed["order"], VMEM),
        "predicted": (fixed["predicted"], VMEM),
        "rel_table": (weights["rel_table"], VMEM),
        "up_bias": (weights["up_bias"], VMEM),
        "biases": (weights["biases"], VMEM),
        "gains": (weights["gains"], VMEM),
        "proj_weight": (weights["proj_weight"], ANY),
        "out_weight": (weights["out_weight"], ANY),
        "up_weight": (weights["up_weight"], ANY),
        "down_weight": (weights["down_weight"], ANY),
        "xc": (xc, ANY),
        "xq": (xq, ANY),
    }
    wide = 2 * rows * micro
    made = {}
    if kept is None:
        made.update(forward_shapes(rows, width, hidden, heads))
    if store is None:
        made.update(
            w_x=shape(wide, width), w_mix_t=shape(width, wide), w_nl=shape(wide, width), w_act=shape(wide, hidden)
        )
    both = 2 * rows
    scratch = [
        pltpu.VMEM((both, width), BF16),
        pltpu.VMEM((3, width, width), BF16),
        pltpu.VMEM((width, width), BF16),
        pltpu.VMEM((width, hidden), BF16),
        pltpu.VMEM((hidden, width), BF16),
        pltpu.VMEM((width, both), BF16),
        pltpu.VMEM((rows, width), BF16),
        pltpu.VMEM((width, rows), BF16),
        pltpu.VMEM((rows, width), BF16),
        pltpu.VMEM((width, rows), BF16),
        pltpu.VMEM((2, rows, rows), F32),
        pltpu.VMEM((16, 2 * rows), F32),
        pltpu.VMEM((2, heads, rows, rows), BF16),
        pltpu.VMEM((2, 16, rows), F32),
        pltpu.VMEM((width, both), BF16),
        pltpu.VMEM((both, width), BF16),
        pltpu.VMEM((both, width), F32),
        pltpu.VMEM((both, width), BF16),
        pltpu.VMEM((both, hidden), BF16),
        pltpu.VMEM((both, hidden), BF16),
        pltpu.VMEM((2, both, width), BF16),
        pltpu.VMEM((2, both, 128), F32),
        pltpu.VMEM((both, width), BF16),
    ]
    buffers = {**(kept or {}), **(store or {})}
    outs = call(fwd_kernel, m, operands, buffers, made, scratch, 8_000_000_000, 32)
    return (
        {n: v for n, v in outs.items() if not n.startswith("w_")},
        {n: v for n, v in outs.items() if n.startswith("w_")},
    )


def backward(m, active, gc, gq, fixed, weights, kept, store, back, made_back):
    rows, width, hidden, heads, micro = fixed["dims"]
    operands = {
        "active": (active, SMEM),
        "rel_table": (weights["rel_table"], VMEM),
        "gains": (weights["gains"], VMEM),
        "proj_weight": (weights["proj_weight"], ANY),
        "out_weight": (weights["out_weight"], ANY),
        "up_weight": (weights["up_weight"], ANY),
        "down_weight": (weights["down_weight"], ANY),
        "gc": (gc, ANY),
        "gq": (gq, ANY),
    }
    for name in ("q_t", "k", "k_t", "v", "e", "inv", "gp", "xhat", "scale"):
        operands[name] = (kept[name], ANY)
    wide = 2 * rows * micro
    both = 2 * rows
    made = {}
    if back is None:
        made.update(
            w_dz=shape(wide, width),
            w_dpre=shape(wide, hidden),
            w_da=shape(wide, width),
            w_dq=shape(wide, width),
            w_dk=shape(wide // 2, width),
            w_dv=shape(wide // 2, width),
        )
    if made_back is None:
        made.update(
            grad=shape(2, rows, width),
            small=shape(8, width, dtype=F32),
            up_small=shape(8, hidden, dtype=F32),
            tab_small=shape(8, heads * BUCKETS, dtype=F32),
        )
    scratch = [
        pltpu.VMEM((both, width), BF16),
        pltpu.VMEM((3, width, width), BF16),
        pltpu.VMEM((width, width), BF16),
        pltpu.VMEM((width, hidden), BF16),
        pltpu.VMEM((hidden, width), BF16),
        pltpu.VMEM((width, both), BF16),
        pltpu.VMEM((rows, width), BF16),
        pltpu.VMEM((width, rows), BF16),
        pltpu.VMEM((rows, width), BF16),
        pltpu.VMEM((2, heads, rows, rows), BF16),
        pltpu.VMEM((2, 16, rows), F32),
        pltpu.VMEM((both, hidden), BF16),
        pltpu.VMEM((2, both, width), BF16),
        pltpu.VMEM((2, both, 128), F32),
        pltpu.VMEM((both, width), F32),
        pltpu.VMEM((both, width), BF16),
        pltpu.VMEM((both, hidden), BF16),
        pltpu.VMEM((both, width), F32),
        pltpu.VMEM((both, width), BF16),
        pltpu.VMEM((width, both), BF16),
        pltpu.VMEM((width, both), BF16),
        pltpu.VMEM((width, rows), BF16),
        pltpu.VMEM((width, rows), BF16),
        pltpu.VMEM((both, width), BF16),
        pltpu.VMEM((rows, width), BF16),
        pltpu.VMEM((rows, width), BF16),
        pltpu.VMEM((16, both), F32),
        pltpu.VMEM((8, width), F32),
        pltpu.VMEM((8, hidden), F32),
        pltpu.VMEM((8, heads * BUCKETS), F32),
        pltpu.VMEM((both, width), BF16),
    ]
    buffers = {**(back or {}), **(made_back or {})}
    outs = call(bwd_kernel, m, operands, buffers, made, scratch, 8_000_000_000, 36)
    return (
        {n: v for n, v in outs.items() if n.startswith("w_")},
        {n: v for n, v in outs.items() if not n.startswith("w_")},
    )


def contract_rows(left, right):
    return jnp.einsum("ra,rb->ab", left, right, preferred_element_type=F32)


def body(
    content_in,
    query_in,
    content_cot,
    query_cot,
    lengths,
    order,
    predicted,
    proj_weight,
    out_weight,
    up_weight,
    down_weight,
    up_bias,
    biases,
    gains,
    rel_table,
):
    micro, rows, width = content_in.shape
    hidden = up_bias.shape[1]
    heads = rel_table.shape[1] // BUCKETS
    first = (lax.axis_index("section") == 0).astype(jnp.int32).reshape(1)
    second = 1 - first
    weights = dict(
        proj_weight=proj_weight,
        out_weight=out_weight,
        up_weight=up_weight,
        down_weight=down_weight,
        up_bias=up_bias,
        biases=biases,
        gains=gains,
        rel_table=rel_table,
    )
    fixed = dict(lengths=lengths, order=order, predicted=predicted, dims=(rows, width, hidden, heads, micro))
    flat = lambda a: a.reshape(micro * rows, width)
    ahead, behind = [(0, 1)], [(1, 0)]
    kept, store, arrived = [None] * micro, None, [None] * micro
    for m in range(micro):
        kept[m], store = forward(m, first, flat(content_in), flat(query_in), fixed, weights, None, store)
        arrived[m] = lax.ppermute(kept[m]["out"], "section", ahead)
    back, made, returned = None, [None] * micro, [None] * micro
    for m in range(micro):
        kept[m], store = forward(m, second, arrived[m][0], arrived[m][1], fixed, weights, kept[m], store)
        back, made[m] = backward(
            m, second, flat(content_cot), flat(query_cot), fixed, weights, kept[m], store, back, None
        )
        returned[m] = lax.ppermute(made[m]["grad"], "section", behind)
    for m in range(micro):
        back, made[m] = backward(
            m, first, returned[m][0], returned[m][1], fixed, weights, kept[m], store, back, made[m]
        )
    half = micro * rows
    down_grad = contract_rows(store["w_act"], back["w_dz"])
    up_grad = contract_rows(store["w_nl"], back["w_dpre"])
    out_grad = jnp.dot(store["w_mix_t"], back["w_da"], preferred_element_type=F32)
    proj_grad = jnp.stack(
        [
            contract_rows(store["w_x"], back["w_dq"]),
            contract_rows(store["w_x"][:half], back["w_dk"]),
            contract_rows(store["w_x"][:half], back["w_dv"]),
        ]
    )
    small = sum(part["small"] for part in made)
    up_small = sum(part["up_small"] for part in made)[0]
    tab_small = sum(part["tab_small"] for part in made)[0]

    def scatter(array, dim):
        array = array.astype(BF16)
        return lax.psum_scatter(array, "dp", scatter_dimension=dim, tiled=True).astype(F32)[None]

    small = scatter(small, 1)
    stack = lambda name, parts, s: jnp.stack([part[name][s] for part in parts])[None]
    return (
        stack("out", kept, 0),
        stack("out", kept, 1),
        stack("grad", made, 0),
        stack("grad", made, 1),
        scatter(proj_grad, 1),
        scatter(out_grad, 0),
        scatter(up_grad, 0),
        scatter(down_grad, 0),
        scatter(up_small, 0),
        small[:, 0:6],
        small[:, 6:8],
        scatter(tab_small, 0),
    )


def solution(mesh):
    return jax.shard_map(
        body,
        mesh=mesh,
        in_specs=(
            P(None, "dp", None),
            P(None, "dp", None),
            P(None, "dp", None),
            P(None, "dp", None),
            P(None, "dp", None),
            P(None, "dp"),
            P(None, "dp"),
            P("section", None, None, None),
            P("section", None, None),
            P("section", None, None),
            P("section", None, None),
            P("section", None),
            P("section", None, None),
            P("section", None, None),
            P("section", None),
        ),
        out_specs=(
            P("section", None, "dp", None),
            P("section", None, "dp", None),
            P("section", None, "dp", None),
            P("section", None, "dp", None),
            P("section", None, "dp", None),
            P("section", "dp", None),
            P("section", "dp", None),
            P("section", "dp", None),
            P("section", "dp"),
            P("section", None, "dp"),
            P("section", None, "dp"),
            P("section", "dp"),
        ),
        check_vma=False,
    )
```

time: 1220 us -> 572 us (0.47)
  matrix products: 334 us -> 26.9 us
  waiting for transfers between devices: 539 us -> 338 us
  local copies, waits for them, and re-layouts: 140 us -> 12.6 us
  Pallas kernels: 0 us -> 119 us
  other arithmetic: 123 us -> 15.2 us
  loops' own time: 17.7 us -> 0 us
    dot_general x114 -> x6, matrix products: 334 us -> 26.9 us  [the longest x5 22.4 us: contract_rows(): return jnp.einsum('ra,rb->ab', left, right, preferred_element_type=F32)]
    reduce_scatter x4, waiting for transfers between devices: 390 us -> 262 us  [scatter(): lax.psum_scatter(array, 'dp', scatter_dimension=dim, tiled=True).astype(F32)]
    pallas_call x0 -> x8, Pallas kernels: none -> 119 us  [call(): pl.pallas_call(partial(kernel, m, names_in, names_out), in_specs=[spec fo...]
    unnamed x10 -> x6, waiting for transfers between devices: 56.1 us -> 0.08 us
    broadcast_in_dim x9, other arithmetic: 42 us -> 10.7 us  [the longest x7 8.14 us: scatter(): lax.psum_scatter(array, 'dp', scatter_dimension=dim, tiled=True).astype(F32)]
    unnamed x302 -> x29, local copies, waits for them, and re-layouts: 35.9 us -> 8.03 us
    cond x258 -> x0, local copies, waits for them, and re-layouts: 24.3 us -> none
    reshape x11 -> x0, local copies, waits for them, and re-layouts: 23.1 us -> none  [the longest x8 22.8 us: layer_forward(): rel_bias = jnp.dot(onehot, table_flat.reshape(32, head_count), precision=...]
  transfers between devices with their start and end apart: 15 -> 9, of which waited for: 9 -> 7; matrix products, arithmetic and copies ran while one was open for 21% -> 8% of each run, Pallas kernels for 0% -> 12%
where the time goes in v1:
time: 572 us; the launch traced here: 566 us
  waiting for transfers between devices  338 us (59%)
  Pallas kernels  119 us (21%)
  blocking collectives  33.1 us (6%)
  matrix products  26.9 us (5%)
  between operations  15.9 us (3%)
  other arithmetic  15.2 us (3%)
  local copies, waits for them, and re-layouts  12.6 us (2%)
  starting transfers between devices  5.76 us (1%)
    reduce_scatter x4, waiting for transfers between devices, scatter(): lax.psum_scatter(array, 'dp', scatter_dimension=dim, tiled=True).astype(F32)  262 us
    pallas_call x8, Pallas kernels, call(): pl.pallas_call(partial(kernel, m, names_in, names_out), in_specs=[spec fo...  119 us
    ppermute x2, waiting for transfers between devices, body(): returned[m] = lax.ppermute(made[m]['grad'], 'section', behind)  66.7 us
    unnamed x1, blocking collectives  33.1 us
    dot_general x5, matrix products, contract_rows(): return jnp.einsum('ra,rb->ab', left, right, preferred_element_type=F32)  22.4 us
  transfers between devices with their start and end apart: 9, of which 7 were waited for; matrix products, arithmetic and copies ran while one was open for 8% of the time, Pallas kernels for 12%

profile of v1, /device:TPU:0, one launch (start us, length us, event | category | flops | bytes accessed | tf_op | source)
XLA Modules:
  0.0 565.8 jit_solution(8509372830294377288)
XLA Ops:
  8.6 26.6 %shard_map.238 = (bf16[768,512]{1,0:T(8,128)(2,1)}, bf16[256,768]{1,0:T(8,128)(2,1)}, bf16[768,256]{1,0:T(8,128)(2,1)}, bf16[256,768]{1,0:T(8,128)(2,1)}, bf16[2...) custom-call(s32[1]{0:T(128)} %bitcast.refs_0_, ...), custom_call_target="tpu_custom_call" | custom-call | flops 8000000000 | bytes 30000000 | tf_op jit(solution)/shard_map/pallas_call | solution.py:457
  36.5 26.9 %shard_map.239 = (bf16[1024,768]{1,0:T(8,128)(2,1)}, bf16[768,1024]{1,0:T(8,128)(2,1)}, bf16[1024,768]{1,0:T(8,128)(2,1)}, bf16[1024,3072]{1,0:T(8,128)(2,1)}, b...) custom-call(s32[1]{0:T(128)} %bitcast.refs_0_, ...), custom_call_target="tpu_custom_call", output_to_operand_aliasing={{0}: (14, {}), {1}: (15, {}), {2}: (16, {}), {3}: (17, {})} | custom-call | flops 8000000000 | bytes 30000000 | tf_op jit(solution)/shard_map/pallas_call | solution.py:457
  67.2 5.1 shard_map.242
  73.6 9.2 %collective-permute-done.1 = bf16[2,256,768]{2,1,0:T(8,128)(2,1)S(1)} collective-permute-done((bf16[2,256,768]{2,1,0:T(8,128)(2,1)}, bf16[2,256,768]{2,1,0:T(8,128)(2,1)S(1)}, u32[]{:S(2)}, u32[]{:S(2)}) %collective-permute-start.1) | collective-permute-done | bytes 786464 | tf_op jit(solution)/shard_map/ppermute | solution.py:666
  83.7 1.6 shard_map.241
  85.3 5.0 shard_map.243
  91.7 38.2 %collective-permute-done.2 = bf16[2,256,768]{2,1,0:T(8,128)(2,1)S(1)} collective-permute-done((bf16[2,256,768]{2,1,0:T(8,128)(2,1)}, bf16[2,256,768]{2,1,0:T(8,128)(2,1)S(1)}, u32[]{:S(2)}, u32[]{:S(2)}) %collective-permute-start.2) | collective-permute-done | bytes 786464 | tf_op jit(solution)/shard_map/ppermute | solution.py:673
  130.8 25.9 %shard_map.244 = (bf16[1024,768]{1,0:T(8,128)(2,1)}, bf16[1024,3072]{1,0:T(8,128)(2,1)}, bf16[1024,768]{1,0:T(8,128)(2,1)}, bf16[1024,768]{1,0:T(8,128)(2,1)}, b...) custom-call(s32[1]{0:T(128)} %bitcast.refs_0_, ...), custom_call_target="tpu_custom_call", output_to_operand_aliasing={{0}: (18, {}), {1}: (19, {}), {2}: (20, {}), {3}: (21, {}),... | custom-call | flops 8000000000 | bytes 30000000 | tf_op jit(solution)/shard_map/pallas_call | solution.py:457
  156.7 28.6 %collective-permute-done.3 = bf16[2,256,768]{2,1,0:T(8,128)(2,1)S(1)} collective-permute-done((bf16[2,256,768]{2,1,0:T(8,128)(2,1)}, bf16[2,256,768]{2,1,0:T(8,128)(2,1)S(1)}, u32[]{:S(2)}, u32[]{:S(2)}) %collective-permute-start.3) | collective-permute-done | bytes 786464 | tf_op jit(solution)/shard_map/ppermute | solution.py:673
  186.2 26.1 %shard_map.245 = (bf16[1024,768]{1,0:T(8,128)(2,1)}, bf16[1024,3072]{1,0:T(8,128)(2,1)}, bf16[1024,768]{1,0:T(8,128)(2,1)}, bf16[1024,768]{1,0:T(8,128)(2,1)}, b...) custom-call(s32[1]{0:T(128)} %bitcast.refs_0_, ...), custom_call_target="tpu_custom_call", output_to_operand_aliasing={{0}: (18, {}), {1}: (19, {}), {2}: (20, {}), {3}: (21, {}),... | custom-call | flops 8000000000 | bytes 30000000 | tf_op jit(solution)/shard_map/pallas_call | solution.py:457
  214.0 4.5 convolution_convert_fusion.2
  221.1 1.5 fusion
  222.5 2.0 pad_maximum_fusion
  225.9 9.8 %convolution_convert_fusion = bf16[3072,768]{1,0:T(8,128)(2,1)} fusion(bf16[1024,3072]{1,0:T(8,128)(2,1)} %get-tuple-element.196, bf16[1024,768]{1,0:T(8,128)(2,1)S(1)} %copy-done), kind=kOutput, calls=%fused_computation | convolution fusion | flops 4834197504 | bytes 12582912 | tf_op jit(solution)/shard_map/ra,rb->ab/dot_general | solution.py:625
  237.1 9.6 %convolution_convert_fusion.1 = bf16[768,3072]{1,0:T(8,128)(2,1)} fusion(bf16[1024,768]{1,0:T(8,128)(2,1)S(1)} %copy-done.5, bf16[1024,3072]{1,0:T(8,128)(2,1)} %get-tuple-element.195), kind=kOutput, calls=%fused_computation.1 | convolution fusion | flops 4834197504 | bytes 12582912 | tf_op jit(solution)/shard_map/ra,rb->ab/dot_general | solution.py:625
  252.4 33.1 %all-reduce.2 = (bf16[3072]{0:T(1024)(128)(2,1)S(1)}, bf16[384]{0:T(512)(128)(2,1)S(1)}) all-reduce(bf16[3072]{0:T(1024)(128)(2,1)S(1)} %fusion.6, bf16[384]{0:T(512)(128)(2,1)S(1)} %fusion.8), channel_id=6, replica_groups=mesh['section'=2,'dp'=16] {'dp'}, use_global_device_ids=true, to_apply=%region_4.0.clone | all-reduce | flops 3456 | bytes 13824
  290.1 38.8 %reduce-scatter.10.cloned.1.call-done = bf16[48,768]{1,0:T(8,128)(2,1)} async-done(((bf16[768,768]{1,0:T(8,128)(2,1)}), bf16[48,768]{1,0:T(8,128)(2,1)}) %reduce-scatter.10.cloned.1.call-update) | async-done | bytes 73744 | tf_op jit(solution)/shard_map/reduce_scatter | solution.py:695
  328.9 1.6 bitcast_convert_fusion.3
  330.5 69.4 %reduce-scatter.8.cloned.1.call-done = bf16[3,48,768]{2,1,0:T(8,128)(2,1)} async-done(((bf16[3,768,768]{2,1,0:T(8,128)(2,1)}), bf16[3,48,768]{2,1,0:T(8,128)(2,1)}) %reduce-scatter.8.cloned.1.call-update) | async-done | bytes 221200 | tf_op jit(solution)/shard_map/reduce_scatter | solution.py:695
  399.9 1.7 bitcast_convert_fusion.2
  401.6 76.5 %reduce-scatter.14.cloned.1.call-done = bf16[192,768]{1,0:T(8,128)(2,1)} async-done(((bf16[3072,768]{1,0:T(8,128)(2,1)}), bf16[192,768]{1,0:T(8,128)(2,1)}) %reduce-scatter.14.cloned.1.call-update) | async-done | bytes 294928 | tf_op jit(solution)/shard_map/reduce_scatter | solution.py:695
  478.1 1.8 bitcast_convert_fusion
  479.9 77.0 %reduce-scatter.12.cloned.1.call-done = bf16[48,3072]{1,0:T(8,128)(2,1)} async-done(((bf16[768,3072]{1,0:T(8,128)(2,1)}), bf16[48,3072]{1,0:T(8,128)(2,1)}) %reduce-scatter.12.cloned.1.call-update) | async-done | bytes 294928 | tf_op jit(solution)/shard_map/reduce_scatter | solution.py:695
  556.9 1.8 bitcast_convert_fusion.1
  (65 shorter events, 27.8 us)
Async XLA Ops:
  7.2 281.0 %reduce-scatter.16.cloned.1.call-start = ((), (), s32[]{:S(2)}) async-start(), calls=%async_computation.9 | async-start | bytes 208896
  35.2 29.6 %collective-permute-start = (bf16[2,256,768]{2,1,0:T(8,128)(2,1)}, bf16[2,256,768]{2,1,0:T(8,128)(2,1)S(1)}, u32[]{:S(2)}, u32[]{:S(2)}) collective-permute-start(bf16[2,256,768]{2,1,0:T(8,128)(2,1)} %get-tuple-element.108.refs_23_), channel_id=1, source_target_pairs={{0,16},{1,17},{2,18},{3,19},{4,20},{5,21},{6,22},{7,23},{8,24},{9,... | collective-permute-start | bytes 2359304 | tf_op jit(solution)/shard_map/ppermute | solution.py:666
  63.5 19.3 %collective-permute-start.1 = (bf16[2,256,768]{2,1,0:T(8,128)(2,1)}, bf16[2,256,768]{2,1,0:T(8,128)(2,1)S(1)}, u32[]{:S(2)}, u32[]{:S(2)}) collective-permute-start(bf16[2,256,768]{2,1,0:T(8,128)(2,1)} %get-tuple-element.127.refs_23_), channel_id=1, source_target_pairs={{0,16},{1,17},{2,18},{3,19},{4,20},{5,21},{6,22},{7,23},{8,24},{9,... | collective-permute-start | bytes 2359304 | tf_op jit(solution)/shard_map/ppermute | solution.py:666
  72.3 57.5 %collective-permute-start.2 = (bf16[2,256,768]{2,1,0:T(8,128)(2,1)}, bf16[2,256,768]{2,1,0:T(8,128)(2,1)S(1)}, u32[]{:S(2)}, u32[]{:S(2)}) collective-permute-start(bf16[2,256,768]{2,1,0:T(8,128)(2,1)} %get-tuple-element.151.refs_24_), channel_id=1, source_target_pairs={{16,0},{17,1},{18,2},{19,3},{20,4},{21,5},{22,6},{23,7},{24,8},{25... | collective-permute-start | bytes 2359304 | tf_op jit(solution)/shard_map/ppermute | solution.py:673
  90.4 95.0 %collective-permute-start.3 = (bf16[2,256,768]{2,1,0:T(8,128)(2,1)}, bf16[2,256,768]{2,1,0:T(8,128)(2,1)S(1)}, u32[]{:S(2)}, u32[]{:S(2)}) collective-permute-start(bf16[2,256,768]{2,1,0:T(8,128)(2,1)} %get-tuple-element.177.refs_24_), channel_id=1, source_target_pairs={{16,0},{17,1},{18,2},{19,3},{20,4},{21,5},{22,6},{23,7},{24,8},{25... | collective-permute-start | bytes 2359304 | tf_op jit(solution)/shard_map/ppermute | solution.py:673
  186.2 26.1 %copy-start.10 = (f32[8,768]{1,0:T(8,128)S(1)}, f32[8,768]{1,0:T(8,128)}, u32[]{:S(2)}) copy-start(f32[8,768]{1,0:T(8,128)} %get-tuple-element.200) | copy-start | bytes 73732
  213.9 115.0 %reduce-scatter.10.cloned.1.call-start = ((), (), s32[]{:S(2)}) async-start(), calls=%async_computation.6 | async-start | bytes 1253376 | tf_op jit(solution)/shard_map/reduce_scatter | solution.py:695
  213.9 4.5 copy-start.2
  214.0 4.5 copy-start.4
  218.4 181.4 %reduce-scatter.8.cloned.1.call-start = ((), (), s32[]{:S(2)}) async-start(), calls=%async_computation.5 | async-start | bytes 3760128 | tf_op jit(solution)/shard_map/reduce_scatter | solution.py:695
  218.5 1.1 copy-start.3
  219.6 1.4 copy-start.1
  224.5 1.4 copy-start
  224.5 253.6 %reduce-scatter.14.cloned.1.call-start = ((), (), s32[]{:S(2)}) async-start(), calls=%async_computation.8 | async-start | bytes 5013504 | tf_op jit(solution)/shard_map/reduce_scatter | solution.py:695
  235.7 1.4 copy-start.5
  235.7 321.2 %reduce-scatter.12.cloned.1.call-start = ((), (), s32[]{:S(2)}) async-start(), calls=%async_computation.7 | async-start | bytes 5013504 | tf_op jit(solution)/shard_map/reduce_scatter | solution.py:695
  246.7 0.7 copy-start.11
  246.7 2.5 copy-start.9
  246.7 2.6 copy-start.6
  249.4 37.4 %copy-start.7 = (bf16[2,256,768]{2,1,0:T(8,128)(2,1)S(1)}, bf16[2,256,768]{2,1,0:T(8,128)(2,1)}, u32[]{:S(2)}) copy-start(bf16[2,256,768]{2,1,0:T(8,128)(2,1)} %get-tuple-element.176) | copy-start | bytes 2359300
  250.6 36.2 %copy-start.8 = (bf16[2,256,768]{2,1,0:T(8,128)(2,1)S(1)}, bf16[2,256,768]{2,1,0:T(8,128)(2,1)}, u32[]{:S(2)}) copy-start(bf16[2,256,768]{2,1,0:T(8,128)(2,1)} %get-tuple-element.187) | copy-start | bytes 2359300
Sparse Core Ops, SparseCore 0:
  214.0 54.1 reduce-scatter.15
  271.9 57.0 reduce-scatter.9
  332.8 67.0 reduce-scatter.7
  403.6 74.4 reduce-scatter.13
  482.3 74.5 reduce-scatter.11
